TPU v7x, 128 devices: a whole 4x4x4 slice. The times are simulated.
128 devices in a mesh: seq: 32 (over z, x_lo, y), head: 4 (over x_hi, core).
Axes of the slice: x: 4 (x_hi: 2, x_lo: 2; x = x_hi * 2 + x_lo), y: 4, z: 4, core: 2. Of those that a mesh axis runs over, the one named last changes fastest.
Arguments:
- queries: bfloat16 [2, 4096, 3584], P(None, 'seq', 'head')
- fine_keys: bfloat16 [2, 4096, 3584], P(None, 'seq', 'head')
- fine_values: bfloat16 [2, 4096, 3584], P(None, 'seq', 'head'), may hold values from -48 to 48
- cache_keys: bfloat16 [2, 1024, 3584], P(None, ('seq', 'head')), may hold values from -6 to 6
- cache_values: bfloat16 [2, 1024, 3584], P(None, ('seq', 'head')), may hold values from -48 to 48
- prefix_len: int32 [2], replicated, may hold values from 512 to 1024, as said below
- out_weight: bfloat16 [3584, 3584], P('head'), may hold values from -0.375 to 0.375
Outputs:
- projected: bfloat16 [2, 4096, 3584], P(None, 'seq', 'head')
Inputs may be any that keep to these rules, and one draw needn't show every extreme that they name: `prefix_len`: the first request sees all 1024 cached tokens.
All inputs are finite; a program needn't handle non-finite values.
Results may differ from a plain program's by a relative error of at most 0.015.
Values may be sent and summed in bfloat16 or wider, within the bound.
A program may use at most 192 MiB of HBM per device.

v0:
```python
import functools

import jax
import jax.numpy as jnp
from jax import lax
from jax.experimental import pallas as pl
from jax.experimental.pallas import tpu as pltpu
from jax.sharding import PartitionSpec as P

MESH = pl.DeviceIdType.MESH
F32, BF = jnp.float32, jnp.bfloat16
HD = 128
HEADS = 7
GW = HEADS * HD
TOK = 128
COARSE = 1024
KEYS = 5120
TQ = 256
CK = 1024
SLOTS = 16
QUART = TOK // 4
PARTS = ((0, 32), (32, 32), (64, 64))
PHASES = ((0, 32), (32, 64), (96, 32))
LOG2 = float(HD ** -0.5 * 1.4426950408889634)


def rcopy(src, dst, ssem, rsem, s, g):
    return pltpu.make_async_remote_copy(
        src_ref=src, dst_ref=dst, send_sem=ssem, recv_sem=rsem,
        device_id=(s, g), device_id_type=MESH)


def kernel(q_ref, fk_ref, fv_ref, ck_ref, cv_ref, plen_ref, w_ref, out_ref,
           st1k, st1v, st2k, st2v, kall, vx, kt, qland, sc0, sc1, qx, mx, acc, obuf, att, wv,
           psend, precv, csend,
           st1_ss, st1_rs, k_ss, k_rs, v_ss, v_rs, q_ss, q_rs, fk_ss, fk_rs, fv_ss, fv_rs,
           ck_ss, ck_rs, cv_ss, cv_rs, cf_ss, cf_rs, o_ss, o_rs, p_ss, p_rs, c_ss, c_rs, w_sem):
    s = lax.axis_index("seq")
    g = lax.axis_index("head")
    z, xl, y = s >> 3, (s >> 2) & 1, s & 3
    xh, c = g >> 1, g & 1
    zk = z >> 1
    land = y & 1
    sib = xh * 2 + 1 - c
    flip = z * 8 + (1 - xl) * 4 + y

    def place(zd, pos):
        return (pos + 8 - 2 * zd) & 7

    def dest(j):
        zb, xb, yb = j >> 3, (j >> 2) & 1, j & 3
        r = (z + zb) & 1
        zd = 2 * c + r
        pos = ((xl + xb) & 1) * 4 + ((y + yb) & 3)
        h = place(zd, pos)
        sd = zd * 8 + pos
        mine = jnp.logical_and(sd == s, land == c)
        return r, h, sd, mine

    my_r = z & 1
    my_h = place(z, xl * 4 + y)
    active = my_h < HEADS

    def slot_of(j):
        return (z >> 1) * 8 + (j >> 3) * 4 + ((j >> 2) & 1) * 2 + ((j & 3) >> 1)

    def source(slot):
        zs = (slot >> 3) * 2 + ((my_r + (slot >> 2)) & 1)
        yb = (slot & 1) * 2 + ((y + c) & 1)
        return zs, (xl + (slot >> 1)) & 1, (y + 4 - yb) & 3

    barrier = pltpu.get_barrier_semaphore()
    gd = xh * 2 + land
    go = xh * 2 + zk

    def greet(j, carry):
        _, _, sd, mine = dest(j)
        zs, xs, ys = source(j)
        ss = zs * 8 + xs * 4 + ys

        @pl.when(jnp.logical_not(mine))
        def _():
            pl.semaphore_signal(barrier, inc=1, device_id=(sd, gd), device_id_type=MESH)

        @pl.when(jnp.logical_not(jnp.logical_and(ss == s, zk == c)))
        def _():
            pl.semaphore_signal(barrier, inc=1, device_id=(ss, go), device_id_type=MESH)
        return carry
    lax.fori_loop(0, 16, greet, 0)
    own = jnp.logical_and(zk == c, land == c)
    for i in range(1, 4):
        pl.semaphore_signal(barrier, inc=1, device_id=(s, (g + i) & 3), device_id_type=MESH)
    for i in range(2):
        pl.semaphore_signal(barrier, inc=1, device_id=(flip, i * 2 + c), device_id_type=MESH)
    wcopy = pltpu.make_async_copy(w_ref, wv, w_sem)
    wcopy.start()
    vx[:, HD:] = jnp.ones((KEYS, HD), BF)
    pl.semaphore_wait(barrier, 37 - jnp.where(own, 2, 0))


    def st1(i, src, dst, n):
        gp = (g + i) & 3
        cols = pl.ds(pl.multiple_of(gp * GW, HD), GW)
        if i == 0:
            return pltpu.make_async_copy(src.at[:, cols], dst.at[g], st1_rs.at[n, 0])
        return rcopy(src.at[:, cols], dst.at[g], st1_ss.at[n, i], st1_rs.at[n, i], s, gp)
    first = [st1(i, src, dst, n) for i in range(4)
             for n, (src, dst) in enumerate(((ck_ref, st1k), (cv_ref, st1v)))]
    for f in first:
        f.start()

    def move(src, dst, ss, rs, sd, mine, gd=gd):
        @pl.when(mine)
        def _():
            pltpu.make_async_copy(src, dst, rs).start()

        @pl.when(jnp.logical_not(mine))
        def _():
            rcopy(src, dst, ss, rs, sd, gd).start()

    has_mine = jnp.logical_and(own, active)

    def sent(piece, n, sem):
        @pl.when(has_mine)
        def _():
            rcopy(piece(n - 1), piece(n - 1), sem, sem, s, sib).wait_send()

        @pl.when(jnp.logical_not(has_mine))
        def _():
            rcopy(piece(n), piece(n), sem, sem, s, sib).wait_send()

    def came(piece, sem):
        rcopy(piece, piece, sem, sem, s, sib).wait_recv()

    def hcols(h):
        return pl.ds(pl.multiple_of(h * HD, HD), HD)

    def krows(slot, n=1):
        return pl.ds(pl.multiple_of(COARSE + slot * TOK, TOK), n * TOK)

    def kv_args(j):
        r, h, sd, mine = dest(j)
        slot = slot_of(j)
        rows = krows(land * 16 + slot)
        return (h, (fk_ref.at[r, :, hcols(h)], kall.at[rows, :], k_ss, k_rs.at[slot >> 2], sd, mine),
                (fv_ref.at[r, :, hcols(h)], vx.at[rows, 0:HD], v_ss, v_rs.at[slot >> 2], sd, mine))

    def q_args(part):
        rows = pl.ds(*PARTS[part])

        def args(j):
            r, h, sd, mine = dest(j)
            slot = slot_of(j)
            return h, (q_ref.at[r, rows, hcols(h)], qland.at[slot, rows, :],
                       q_ss.at[part], q_rs.at[part, slot >> 3], sd, mine)
        return args

    def c_args(j):
        r, h, sd, mine = dest(j)
        spot = land * 16 + z * 4 + xl * 2 + (y >> 1)
        rows = pl.ds(pl.multiple_of(spot * 32, 32), 32)
        return (h, (st2k.at[r, :, hcols(h)], kall.at[rows, :], ck_ss, ck_rs, sd, mine),
                (st2v.at[r, :, hcols(h)], vx.at[rows, 0:HD], cv_ss, cv_rs, sd, mine))

    def each(args, what):
        def step(j, carry):
            h, *copies = args(j)

            @pl.when(h < HEADS)
            def _():
                for a in copies:
                    what(*a)
            return carry
        lax.fori_loop(0, 16, step, 0)

    each(kv_args, move)

    for i in range(4):
        for n, (src, dst) in enumerate(((ck_ref, st1k), (cv_ref, st1v))):
            if i == 0:
                st1(0, src, dst, n).wait()
            else:
                st1(i, src, dst, n).wait_recv()
    for r in range(2):
        for a in range(2):
            for src, dst in ((st1k, st2k), (st1v, st2v)):
                lo = src[2 * a].astype(F32)[r * 8:r * 8 + 8]
                hi = src[2 * a + 1].astype(F32)[r * 8:r * 8 + 8]
                dst[r, a * 16:a * 16 + 16, :] = jnp.concatenate([lo, hi], axis=0).astype(BF)
    each(c_args, move)
    each(q_args(0), move)

    ohead = pl.multiple_of(my_h * HD, HD)

    def o_args(ph, j):
        zs, xs, ys = source(j)
        so = zs * 8 + (1 - xs) * 4 + ys
        rows = pl.ds(*PHASES[ph])
        mine = jnp.logical_and(so == s, zk == c)
        return (obuf.at[j, rows, :], att.at[my_r, rows, pl.ds(ohead, HD)], o_ss.at[ph],
                o_rs.at[ph], so, mine, go)

    def give_back(ph, first, count):
        def step(j, carry):
            move(*o_args(ph, j))
            return carry
        lax.fori_loop(first, first + count, step, 0)

    def fwd(ref_k, ss, rs, i, owner, is_v):
        rows = krows(owner * 16 + i * 4, 4)
        piece = ref_k.at[rows, 0:HD] if is_v else ref_k.at[rows, :]
        return rcopy(piece, piece, ss.at[i], rs.at[i], s, sib)

    def cfwd(ref_k, n, owner, is_v):
        rows = pl.ds(pl.multiple_of(owner * 512, 512), 512)
        piece = ref_k.at[rows, 0:HD] if is_v else ref_k.at[rows, :]
        return rcopy(piece, piece, cf_ss.at[n], cf_rs.at[n], s, sib)

    def transpose(row):
        for b in range(2):
            rows = pl.ds(pl.multiple_of(row + b * 256, 256), 256)
            kk = kall[rows, :].T
            kt[0:HD, rows] = kk
            kt[HD:, rows] = kk

    @pl.when(active)
    def _():
        def landed(i, carry):
            rows = krows(c * 16 + i * 4, 4)
            came(kall.at[rows, :], k_rs.at[i])
            fwd(kall, fk_ss, fk_rs, i, c, False).start()
            came(vx.at[rows, 0:HD], v_rs.at[i])
            fwd(vx, fv_ss, fv_rs, i, c, True).start()
            return carry
        lax.fori_loop(0, 4, landed, 0)
        rows = pl.ds(pl.multiple_of(c * 512, 512), 512)
        came(kall.at[rows, :], ck_rs)
        cfwd(kall, 0, c, False).start()
        came(vx.at[rows, 0:HD], cv_rs)
        cfwd(vx, 1, c, True).start()

    sent(lambda n: kall.at[0:n * TOK, :], 14, k_ss)
    sent(lambda n: kall.at[0:n * TOK, :], 14, v_ss)
    each(q_args(1), move)
    each(q_args(2), move)

    scs = (sc0, sc1)

    def prep(quart, half):
        slots = pl.ds(half * 8, 8)

        for b in range(len(PARTS)):
            @pl.when(quart == PARTS[b][0] // QUART)
            def _():
                came(qland.at[slots, pl.ds(*PARTS[b]), :], q_rs.at[b, half])
        rows = pl.ds(pl.multiple_of(quart * QUART, QUART), QUART)
        x = qland[half * 8:half * 8 + 8, rows, :].reshape(TQ, HD).astype(F32) * LOG2
        hi = x.astype(BF)
        qx[:, :HD] = hi
        qx[:, HD:] = (x - hi.astype(F32)).astype(BF)
        mx[...] = jnp.full((TQ, HD), -jnp.inf, F32)

    def qk(cols, sc):
        val = jnp.dot(qx[...], kt[:, cols], preferred_element_type=F32)
        sc[:, cols] = val
        m = mx[...]
        for b in range(CK // HD):
            m = jnp.maximum(m, val[:, b * HD:(b + 1) * HD])
        mx[...] = m

    @pl.when(active)
    def _():
        def mine_t(i, carry):
            transpose(COARSE + c * 2048 + i * 512)
            return carry
        lax.fori_loop(0, 4, mine_t, 0)
        prep(0, 0)

        def early(owner):
            def step(i, carry):
                qk(pl.ds(pl.multiple_of(COARSE + owner * 2048 + i * CK, CK), CK), sc0)
                return carry
            lax.fori_loop(0, 2, step, 0)
        early(c)

        def theirs_t(i, carry):
            fwd(kall, fk_ss, fk_rs, i, 1 - c, False).wait_recv()
            transpose(COARSE + (1 - c) * 2048 + i * 512)
            return carry
        lax.fori_loop(0, 4, theirs_t, 0)
        early(1 - c)

        def theirs_v(i, carry):
            fwd(vx, fv_ss, fv_rs, i, 1 - c, True).wait_recv()
            fwd(kall, fk_ss, fk_rs, i, c, False).wait_send()
            fwd(vx, fv_ss, fv_rs, i, c, True).wait_send()
            return carry
        lax.fori_loop(0, 4, theirs_v, 0)
        cfwd(kall, 0, 1 - c, False).wait_recv()
        cfwd(vx, 1, 1 - c, True).wait_recv()
        cfwd(kall, 0, c, False).wait_send()
        cfwd(vx, 1, c, True).wait_send()

        plen = plen_ref[my_r]
        k0 = kall[COARSE:COARSE + 1, :].astype(F32)
        row = lax.broadcasted_iota(jnp.int32, (256, HD), 0)
        token = 512 + (row >> 6) * 128 + ((row >> 5) & 1) * 64 + (row & 31)
        for i in range(4):
            rows = slice(i * 256, (i + 1) * 256)
            kk = kall[rows, :]
            if i % 2 == 1:
                seen = token + (i // 2) * 32 < plen
                kk = jnp.where(seen, kk.astype(F32), k0).astype(BF)
                vx[rows, 0:HD] = jnp.where(seen, vx[rows, 0:HD].astype(F32), 0.0).astype(BF)
                vx[rows, HD:] = jnp.where(seen, 1.0, 0.0).astype(BF)
            kk = kk.T
            kt[0:HD, rows] = kk
            kt[HD:, rows] = kk
        qk(slice(0, COARSE), sc0)

    def part(ph, gp):
        r0, n = PHASES[ph]
        rows = jnp.concatenate([att[0, r0:r0 + n, :], att[1, r0:r0 + n, :]], axis=0)
        cols = pl.ds(pl.multiple_of(gp * GW, HD), GW)
        return jnp.dot(rows, wv[:, cols], preferred_element_type=F32)

    def pcopy(ph, i):
        rows = pl.ds(2 * PHASES[ph][0], 2 * PHASES[ph][1])
        return rcopy(psend.at[i, rows, :], precv.at[i, rows, :], p_ss.at[ph, i], p_rs.at[ph, i], s, sib)

    def ccopy(ph, i, half):
        rows = pl.ds(*PHASES[ph])
        return rcopy(csend.at[i, :, rows, :], out_ref.at[half, :, rows, :], c_ss.at[ph, i],
                     c_rs.at[ph, half], flip, i * 2 + c)

    def give(ph):
        r0, n = PHASES[ph]

        came(att.at[:, pl.ds(r0, n), :], o_rs.at[ph])
        if ph == 0:
            wcopy.wait()

        def step(i, carry):
            psend[i, 2 * r0:2 * (r0 + n), :] = part(ph, i * 2 + 1 - c).astype(BF)
            pcopy(ph, i).start()
            return carry
        lax.fori_loop(0, 2, step, 0)

    def take(ph):
        r0, n = PHASES[ph]

        def step(i, carry):
            val = part(ph, i * 2 + c)
            pcopy(ph, i).wait_recv()
            val = (val + precv[i, 2 * r0:2 * (r0 + n), :].astype(F32)).astype(BF)
            for r in range(2):
                csend[i, r, r0:r0 + n, :] = val[r * n:(r + 1) * n]
            ccopy(ph, i, xh).start()
            return carry
        lax.fori_loop(0, 2, step, 0)

    def pv(ci, sc, mrow):
        cols = slice(ci * CK, (ci + 1) * CK)
        p = jnp.exp2(sc[:, cols] - mrow).astype(BF)
        acc[...] += jnp.dot(p, vx[cols, :], preferred_element_type=F32)

    def tile(quart, half, final=False):
        mrow = jnp.max(mx[...], axis=1, keepdims=True)
        acc[...] = jnp.zeros((TQ, 2 * HD), F32)
        if not final:
            prep(quart + half, 1 - half)
        for ci in range(KEYS // CK):
            if not final:
                qk(slice(ci * CK, (ci + 1) * CK), scs[1 - half])
            pv(ci, scs[half], mrow)
        o = (acc[:, :HD] / acc[:, HD:]).astype(BF)
        rows = pl.ds(pl.multiple_of(quart * QUART, QUART), QUART)
        obuf[half * 8:half * 8 + 8, rows, :] = o.reshape(8, QUART, HD)

    def quarter(quart, carry):
        @pl.when(active)
        def _():
            tile(quart, 0)

        @pl.when(quart == 2)
        def _():
            give(0)

        @pl.when(active)
        def _():
            tile(quart, 1)

            @pl.when(quart == 0)
            def _():
                give_back(0, 0, 16)

            @pl.when(quart == 2)
            def _():
                give_back(1, 0, 16)
        return carry
    lax.fori_loop(0, 3, quarter, 0)
    take(0)

    @pl.when(active)
    def _():
        tile(3, 0)
        give_back(2, 0, 8)
        tile(3, 1, True)
        give_back(2, 8, 8)
    give(1)
    take(1)
    for i in range(1, 4):
        for n, (src, dst) in enumerate(((ck_ref, st1k), (cv_ref, st1v))):
            st1(i, src, dst, n).wait_send()
    sent(lambda n: kall.at[0:n * 32, :], 14, ck_ss)
    sent(lambda n: kall.at[0:n * 32, :], 14, cv_ss)
    for b in range(len(PARTS)):
        sent(lambda n: qland.at[0:n, pl.ds(*PARTS[b]), :], 14, q_ss.at[b])
    give(2)
    take(2)

    @pl.when(active)
    def _():
        for ph in range(len(PHASES)):
            sent(lambda n: obuf.at[0:n, pl.ds(*PHASES[ph]), :], 16, o_ss.at[ph])
    for ph in range(len(PHASES)):
        for i in range(2):
            pcopy(ph, i).wait_send()
            ccopy(ph, i, xh).wait_send()
    for ph in range(len(PHASES)):
        for i in range(2):
            ccopy(ph, i, i).wait_recv()


def per_device(queries, fine_keys, fine_values, cache_keys, cache_values, prefix_len, out_weight):
    dma = pltpu.SemaphoreType.DMA
    any_spec = pl.BlockSpec(memory_space=pl.ANY)
    halves = pl.pallas_call(
        kernel,
        out_shape=jax.ShapeDtypeStruct((2, 2, TOK, GW), BF),
        in_specs=[any_spec] * 5 + [pl.BlockSpec(memory_space=pltpu.SMEM), any_spec],
        out_specs=any_spec,
        scratch_shapes=[
            pltpu.VMEM((4, 16, GW), BF), pltpu.VMEM((4, 16, GW), BF),
            pltpu.VMEM((2, 32, GW), BF), pltpu.VMEM((2, 32, GW), BF),
            pltpu.VMEM((KEYS, HD), BF), pltpu.VMEM((KEYS, 2 * HD), BF),
            pltpu.VMEM((2 * HD, KEYS), BF), pltpu.VMEM((SLOTS, TOK, HD), BF),
            pltpu.VMEM((TQ, KEYS), F32), pltpu.VMEM((TQ, KEYS), F32),
            pltpu.VMEM((TQ, 2 * HD), BF), pltpu.VMEM((TQ, HD), F32),
            pltpu.VMEM((TQ, 2 * HD), F32), pltpu.VMEM((SLOTS, TOK, HD), BF),
            pltpu.VMEM((2, TOK, GW), BF), pltpu.VMEM((GW, 4 * GW), BF),
            pltpu.VMEM((2, 2 * TOK, GW), BF), pltpu.VMEM((2, 2 * TOK, GW), BF),
            pltpu.VMEM((2, 2, TOK, GW), BF),
            dma((2, 4)), dma((2, 4)), dma, dma((4,)), dma, dma((4,)),
            dma((3,)), dma((3, 2)), dma((4,)), dma((4,)), dma((4,)), dma((4,)),
            dma, dma, dma, dma, dma((2,)), dma((2,)),
            dma((3,)), dma((3,)), dma((3, 2)), dma((3, 2)), dma((3, 2)), dma((3, 2)), dma,
        ],
        compiler_params=pltpu.CompilerParams(
            collective_id=0, has_side_effects=True, vmem_limit_bytes=58 * 2**20),
        cost_estimate=pl.CostEstimate(flops=7_000_000_000, bytes_accessed=12_000_000, transcendentals=10_000_000),
    )(queries, fine_keys, fine_values, cache_keys.reshape(16, 4 * GW),
      cache_values.reshape(16, 4 * GW), prefix_len, out_weight)
    return (halves[0].astype(F32) + halves[1].astype(F32)).astype(BF)


def solution(mesh):
    return jax.shard_map(
        per_device,
        mesh=mesh,
        in_specs=(
            P(None, "seq", "head"),
            P(None, "seq", "head"),
            P(None, "seq", "head"),
            P(None, ("seq", "head"), None),
            P(None, ("seq", "head"), None),
            P(),
            P("head", None),
        ),
        out_specs=P(None, "seq", "head"),
        check_vma=False,
    )
```

profile of v0, /device:TPU:1, one launch (start us, length us, event | category | flops | bytes accessed | tf_op | source)
XLA Modules:
  0.0 64.0 jit_solution(15212308274160523042)
XLA Ops:
  0.0 62.0 %shard_map.73 = bf16[2,2,128,896]{3,2,1,0:T(8,128)(2,1)} custom-call(bf16[2,128,896]{2,1,0:T(8,128)(2,1)} %q_ref.1, bf16[2,128,896]{2,1,0:T(8,128)(2,1)} %fk_ref.1, bf16[2,128,896]{2,1,0:T(8,128)(2,1)} %fv_ref.1, bf16[16,3584]{1,0:T(8,128)(2,1)} %bitcast.4, bf16[16,3584]{1,0:T(8,128)(2,1)} %bitcast.5, s32[2]{0:T(128)} %plen_ref.1, bf16[896,3584]{1,0:T(8,128)(2,1)} %w_ref.1), custom_call_target="tpu_custom_call" | custom-call | flops 7000000000 | bytes 12000000 | tf_op jit(solution)/shard_map/pallas_call | solution.py:438
  62.0 2.0 %fusion = bf16[2,128,896]{2,1,0:T(8,128)(2,1)} fusion(bf16[2,2,128,896]{3,2,1,0:T(8,128)(2,1)} %shard_map.73), kind=kLoop, calls=%fused_computation.1 | loop fusion | flops 917504 | bytes 1376256 | tf_op jit(solution)/shard_map/convert_element_type | solution.py:464
where the time goes:
time: 64.3 us; the launch traced here: 64 us
  Pallas kernels  62 us (96%)
  other arithmetic  2.03 us (3%)
    pallas_call x1, Pallas kernels, per_device(): pl.pallas_call(kernel, out_shape=jax.ShapeDtypeStruct((2, 2, TOK, GW), BF...  62 us
    convert_element_type x1, other arithmetic, per_device(): return (halves[0].astype(F32) + halves[1].astype(F32)).astype(BF)  2.03 us

commit v1 on v0

--- a/solution.py
+++ b/solution.py
@@ -73,20 +73,17 @@
     gd = xh * 2 + land
     go = xh * 2 + zk
 
-    def greet(j, carry):
-        _, _, sd, mine = dest(j)
+    def greet(sp, gp, maybe_here):
+        def signal():
+            pl.semaphore_signal(barrier, inc=1, device_id=(sp, gp), device_id_type=MESH)
+        if maybe_here:
+            pl.when(jnp.logical_not(jnp.logical_and(sp == s, gp == g)))(signal)
+        else:
+            signal()
+    for j in range(15, -1, -1):
+        greet(dest(j)[2], gd, j & 7 == 0)
         zs, xs, ys = source(j)
-        ss = zs * 8 + xs * 4 + ys
-
-        @pl.when(jnp.logical_not(mine))
-        def _():
-            pl.semaphore_signal(barrier, inc=1, device_id=(sd, gd), device_id_type=MESH)
-
-        @pl.when(jnp.logical_not(jnp.logical_and(ss == s, zk == c)))
-        def _():
-            pl.semaphore_signal(barrier, inc=1, device_id=(ss, go), device_id_type=MESH)
-        return carry
-    lax.fori_loop(0, 16, greet, 0)
+        greet(zs * 8 + xs * 4 + ys, go, j & 3 == 0)
     own = jnp.logical_and(zk == c, land == c)
     for i in range(1, 4):
         pl.semaphore_signal(barrier, inc=1, device_id=(s, (g + i) & 3), device_id_type=MESH)

time: 64.3 us -> 63.3 us (0.984)
  Pallas kernels: 62 us -> 61 us
    pallas_call x1, Pallas kernels: 62 us -> 61 us  [per_device(): pl.pallas_call(kernel, out_shape=jax.ShapeDtypeStruct((2, 2, TOK, GW), BF...]
where the time goes in v1:
time: 63.3 us; the launch traced here: 63.1 us
  Pallas kernels  61 us (96%)
  other arithmetic  2.03 us (3%)
    pallas_call x1, Pallas kernels, per_device(): pl.pallas_call(kernel, out_shape=jax.ShapeDtypeStruct((2, 2, TOK, GW), BF...  61 us
    convert_element_type x1, other arithmetic, per_device(): return (halves[0].astype(F32) + halves[1].astype(F32)).astype(BF)  2.03 us

profile of v1, /device:TPU:1, one launch (start us, length us, event | category | flops | bytes accessed | tf_op | source)
XLA Modules:
  0.0 63.1 jit_solution(8691192106391272220)
XLA Ops:
  0.0 61.0 %shard_map.73 = bf16[2,2,128,896]{3,2,1,0:T(8,128)(2,1)} custom-call(bf16[2,128,896]{2,1,0:T(8,128)(2,1)} %q_ref.1, bf16[2,128,896]{2,1,0:T(8,128)(2,1)} %fk_ref.1, bf16[2,128,896]{2,1,0:T(8,128)(2,1)} %fv_ref.1, bf16[16,3584]{1,0:T(8,128)(2,1)} %bitcast.4, bf16[16,3584]{1,0:T(8,128)(2,1)} %bitcast.5, s32[2]{0:T(128)} %plen_ref.1, bf16[896,3584]{1,0:T(8,128)(2,1)} %w_ref.1), custom_call_target="tpu_custom_call" | custom-call | flops 7000000000 | bytes 12000000 | tf_op jit(solution)/shard_map/pallas_call | solution.py:435
  61.0 2.0 %fusion = bf16[2,128,896]{2,1,0:T(8,128)(2,1)} fusion(bf16[2,2,128,896]{3,2,1,0:T(8,128)(2,1)} %shard_map.73), kind=kLoop, calls=%fused_computation.1 | loop fusion | flops 917504 | bytes 1376256 | tf_op jit(solution)/shard_map/convert_element_type | solution.py:461
